TPU v7x, 128 devices: a whole 4x4x4 slice. The times are simulated.
128 devices in a mesh: func: 128 (over z, x, y, core).
Axes of the slice: x: 4, y: 4, z: 4, core: 2. Of those that a mesh axis runs over, the one named last changes fastest.
Arguments:
- basis_wavefunctions: bfloat16 [16384, 8, 2048], P('func')
- filling_weights: float32 [16384], P('func'), may hold values from 0.5 to 2
- living_per_unit: int32 [128], replicated, may hold values from 64 to 128, as said below
- starting_sheets: int32 [16384], replicated, may hold values from 0 to 1023, as said below
- nucleus_charge: float32 [1024, 2048], P('func'), may hold values from 0.2 to 2
- applied_field: float32 [1024, 2048], P('func'), may hold values from -2 to 2
Outputs:
- charge_distribution: float32 [1024, 2048], P('func')
- ham: float32 [16384, 384], P('func')
- ovl: float32 [16384, 384], P('func')
Inputs may be any that keep to these rules, and one draw needn't show every extreme that they name: `living_per_unit`: one device holds exactly 128 live functions. `starting_sheets`: slot s of device k starts at plane k * 8 + t with 0 <= t < 8; slot 0 has t = 0 and slot 127 has t = 7.
All inputs are finite; a program needn't handle non-finite values.
Results may differ from a plain program's by a relative error of at most 0.0003.
Values may be sent and summed in bfloat16 or wider, within the bound.
A program may use at most 192 MiB of HBM per device.

v0:
```python
import functools

import jax
import jax.numpy as jnp
from jax import lax
from jax.experimental import pallas as pl
from jax.experimental.pallas import tpu as pltpu
from jax.sharding import PartitionSpec as P

MESH = pl.DeviceIdType.MESH
F32 = jnp.float32
BF16 = jnp.bfloat16

SLOTS = 128
DEPTH = 8
PLANES = 2 * DEPTH - 1
GROUP = 16
GROUPS = SLOTS // GROUP
PIECES = 4


def dot_nt(a, b):
    return lax.dot_general(a, b, (((1,), (1,)), ((), ())), preferred_element_type=F32)


def cube_root(x):
    y = jnp.exp(jnp.log(x) * (1.0 / 3.0))
    return (2.0 * y + x / (y * y)) * (1.0 / 3.0)


def kernel(
    count,
    boxes,
    weights,
    living,
    sheets,
    nucleus,
    applied,
    rho_out,
    ham_out,
    ovl_out,
    raw,
    selector,
    wide_weights,
    stack,
    from_prev,
    from_next,
    dens,
    pot,
    rho,
    up_out,
    up_in,
    down_out,
    down_in,
    own,
    part,
    part_in,
    ham,
    ovl,
    raw_sem,
    down_sems,
    up_sems,
    planes_down_sems,
    planes_up_sems,
    plane_sems,
    part_sems,
    out_sems,
):
    me = lax.axis_index("func")
    following = lax.rem(me + 1, count)
    preceding = lax.rem(me + count - 1, count)
    width = raw.shape[2]

    def points(piece):
        return pl.ds(pl.multiple_of(piece * width, width), width)

    def raw_copy(piece):
        return pltpu.make_async_copy(
            boxes.at[:, points(piece)], raw.at[piece], raw_sem.at[piece]
        )

    for piece in range(PIECES):
        raw_copy(piece).start()

    barrier = pltpu.get_barrier_semaphore()
    for neighbour in (preceding, following):
        pl.semaphore_signal(barrier, inc=1, device_id=(neighbour,), device_id_type=MESH)

    start = (sheets[pl.ds(me, 1), :] - me * DEPTH).astype(F32)
    lane = lax.broadcasted_iota(jnp.int32, (1, SLOTS), 1)
    start = jnp.where(lane < living[me], start, 64.0)
    lanes = lax.broadcasted_iota(jnp.int32, (GROUPS, SLOTS), 1)
    rows = lax.broadcasted_iota(jnp.int32, (GROUPS, SLOTS), 0)
    spread = jnp.where(lanes // GROUP == rows, start, 0.0).astype(BF16)
    repeat = (
        lax.broadcasted_iota(jnp.int32, (SLOTS, SLOTS), 0) % GROUP
        == lax.broadcasted_iota(jnp.int32, (SLOTS, SLOTS), 1) // DEPTH
    )
    column_start = jnp.dot(
        spread, jnp.where(repeat, 1.0, 0.0).astype(BF16), preferred_element_type=F32
    )
    row = lax.broadcasted_iota(jnp.int32, (PLANES * GROUP, SLOTS), 0)
    column = lax.broadcasted_iota(jnp.int32, (PLANES * GROUP, SLOTS), 1)
    offset = jnp.where(
        row % GROUP == column // DEPTH, row // GROUP - column % DEPTH, -99
    ).astype(F32)
    for group in range(GROUPS):
        selector[group] = jnp.where(offset == column_start[group : group + 1, :], 1.0, 0.0).astype(BF16)
    wide_weights[...] = jnp.broadcast_to(weights[...], (SLOTS, SLOTS)).T

    pl.semaphore_wait(barrier, 2)

    def down_copy(piece):
        return pltpu.make_async_remote_copy(
            src_ref=down_out.at[piece],
            dst_ref=down_in.at[piece],
            send_sem=down_sems.at[0, piece],
            recv_sem=down_sems.at[1, piece],
            device_id=(following,),
            device_id_type=MESH,
        )

    def up_copy(piece):
        return pltpu.make_async_remote_copy(
            src_ref=up_out.at[piece],
            dst_ref=up_in.at[piece],
            send_sem=up_sems.at[0, piece],
            recv_sem=up_sems.at[1, piece],
            device_id=(preceding,),
            device_id_type=MESH,
        )

    def planes_down_copy(piece):
        return pltpu.make_async_remote_copy(
            src_ref=stack.at[piece, pl.ds(DEPTH + 4, 3), pl.ds(0, SLOTS), :],
            dst_ref=from_prev.at[piece, pl.ds(1, 3)],
            send_sem=planes_down_sems.at[0, piece],
            recv_sem=planes_down_sems.at[1, piece],
            device_id=(following,),
            device_id_type=MESH,
        )

    def planes_up_copy(piece):
        return pltpu.make_async_remote_copy(
            src_ref=stack.at[piece, pl.ds(0, 3), pl.ds(0, SLOTS), :],
            dst_ref=from_next.at[piece, pl.ds(0, 3)],
            send_sem=planes_up_sems.at[0, piece],
            recv_sem=planes_up_sems.at[1, piece],
            device_id=(preceding,),
            device_id_type=MESH,
        )

    def plane_up_copy(piece):
        return pltpu.make_async_remote_copy(
            src_ref=stack.at[piece, 3, pl.ds(0, SLOTS), :],
            dst_ref=from_next.at[piece, 3],
            send_sem=plane_sems.at[0, piece],
            recv_sem=plane_sems.at[1, piece],
            device_id=(preceding,),
            device_id_type=MESH,
        )

    def plane_down_copy(piece):
        return pltpu.make_async_remote_copy(
            src_ref=stack.at[piece, DEPTH + 3, pl.ds(0, SLOTS), :],
            dst_ref=from_prev.at[piece, 0],
            send_sem=plane_sems.at[0, piece],
            recv_sem=plane_sems.at[1, piece],
            device_id=(following,),
            device_id_type=MESH,
        )

    def place_piece(piece, carry):
        raw_copy(piece).wait()
        dens[...] = jnp.zeros_like(dens)

        def place_group(group, carry):
            slots = pl.ds(pl.multiple_of(group * GROUP, GROUP), GROUP)
            source = raw[piece, pl.ds(pl.multiple_of(group * GROUP * DEPTH, GROUP * DEPTH), GROUP * DEPTH), :]
            placed = jnp.dot(selector[group], source, preferred_element_type=F32)
            placed = placed.reshape(PLANES, GROUP, width)
            stack[piece, :, slots, :] = placed.astype(BF16)
            weight = jnp.concatenate([wide_weights[slots, :]] * (width // SLOTS), axis=1)
            terms = placed * placed * weight[None]
            dens[...] += terms[:, :DEPTH] + terms[:, DEPTH:]
            return carry

        lax.fori_loop(0, GROUPS, place_group, 0)
        down_out[piece] = jnp.zeros_like(down_out[piece])
        down_out[piece, : DEPTH - 1] = jnp.sum(dens[DEPTH:], axis=1)
        up_out[piece, 0] = nucleus[:, points(piece)] + jnp.sum(dens[:DEPTH], axis=1)
        up_out[piece, 1] = applied[:, points(piece)]
        down_copy(piece).start()
        up_copy(piece).start()
        planes_down_copy(piece).start()
        planes_up_copy(piece).start()

        @pl.when(piece < PIECES // 2)
        def _():
            plane_up_copy(piece).start()

        @pl.when(piece >= PIECES // 2)
        def _():
            plane_down_copy(piece).start()

        return carry

    lax.fori_loop(0, PIECES, place_piece, 0)

    own[...] = jnp.zeros_like(own)

    def own_piece(piece, carry):
        down_copy(piece).wait()
        up_copy(piece).wait()
        density = up_out[piece, 0] + down_in[piece]
        rho[:, points(piece)] = density
        pot[piece, :DEPTH] = up_out[piece, 1] - 0.9847 * cube_root(density)
        pot[piece, DEPTH:] = up_in[piece, 1] - 0.9847 * cube_root(up_in[piece, 0] + down_out[piece])
        total = own[...]
        for plane in range(PLANES):
            phi = stack[piece, plane, :SLOTS, :]
            stack[piece, plane, SLOTS:, :] = (phi.astype(F32) * pot[piece, plane : plane + 1, :]).astype(BF16)
            total += dot_nt(phi, stack[piece, plane])
        own[...] = total
        return carry

    lax.fori_loop(0, PIECES, own_piece, 0)
    rho_copy = pltpu.make_async_copy(rho, rho_out, out_sems.at[0])
    rho_copy.start()

    scale = 1.0 / (DEPTH * width * PIECES)
    part[...] = jnp.zeros_like(part)

    def cross_piece(piece, carry):
        planes_up_copy(piece).wait()
        planes_down_copy(piece).wait()
        total = part[0]
        for shared in range(3):
            total += dot_nt(from_next[piece, shared], stack[piece, DEPTH + shared])
        part[0] = total
        total = part[1]
        for shared in range(4, 7):
            total += dot_nt(from_prev[piece, shared - 3], stack[piece, shared])
        part[1] = total

        @pl.when(piece < PIECES // 2)
        def _():
            plane_up_copy(piece).wait()
            part[0] += dot_nt(from_next[piece, 3], stack[piece, DEPTH + 3])

        @pl.when(piece >= PIECES // 2)
        def _():
            plane_down_copy(piece).wait()
            part[1] += dot_nt(from_prev[piece, 0], stack[piece, 3])

        return carry

    lax.fori_loop(0, PIECES, cross_piece, 0)

    def part_copy(side, target):
        return pltpu.make_async_remote_copy(
            src_ref=part.at[side],
            dst_ref=part_in.at[side],
            send_sem=part_sems.at[0, side],
            recv_sem=part_sems.at[1, side],
            device_id=(target,),
            device_id_type=MESH,
        )

    to_next = part_copy(0, following)
    to_prev = part_copy(1, preceding)
    to_next.start()
    to_prev.start()
    ovl[:, SLOTS : 2 * SLOTS] = own[:, :SLOTS] * scale
    ham[:, SLOTS : 2 * SLOTS] = own[:, SLOTS:] * scale
    ovl_next = part[0, :, :SLOTS].T
    ham_next = part[0, :, SLOTS:].T
    ovl_prev = part[1, :, :SLOTS].T
    ham_prev = part[1, :, SLOTS:].T
    to_next.wait()
    to_prev.wait()
    ovl[:, :SLOTS] = (ovl_prev + part_in[0, :, :SLOTS]) * scale
    ham[:, :SLOTS] = (ham_prev + part_in[0, :, SLOTS:]) * scale
    ovl[:, 2 * SLOTS :] = (ovl_next + part_in[1, :, :SLOTS]) * scale
    ham[:, 2 * SLOTS :] = (ham_next + part_in[1, :, SLOTS:]) * scale
    ovl_copy = pltpu.make_async_copy(ovl, ovl_out, out_sems.at[1])
    ham_copy = pltpu.make_async_copy(ham, ham_out, out_sems.at[2])
    ovl_copy.start()
    ham_copy.start()
    rho_copy.wait()
    ovl_copy.wait()
    ham_copy.wait()


def per_device(
    basis_wavefunctions,
    filling_weights,
    living_per_unit,
    starting_sheets,
    nucleus_charge,
    applied_field,
):
    slots, depth, points = basis_wavefunctions.shape
    count = lax.axis_size("func")
    width = points // PIECES
    vmem = pl.BlockSpec(memory_space=pltpu.VMEM)
    anywhere = pl.BlockSpec(memory_space=pl.ANY)
    pair = pltpu.SemaphoreType.DMA((2, PIECES))
    rho, ham, ovl = pl.pallas_call(
        functools.partial(kernel, count),
        out_shape=(
            jax.ShapeDtypeStruct((depth, points), F32),
            jax.ShapeDtypeStruct((slots, 3 * slots), F32),
            jax.ShapeDtypeStruct((slots, 3 * slots), F32),
        ),
        in_specs=[
            anywhere,
            vmem,
            pl.BlockSpec(memory_space=pltpu.SMEM),
            vmem,
            vmem,
            vmem,
        ],
        out_specs=(anywhere, anywhere, anywhere),
        scratch_shapes=[
            pltpu.VMEM((PIECES, slots * depth, width), BF16),
            pltpu.VMEM((GROUPS, PLANES * GROUP, slots), BF16),
            pltpu.VMEM((slots, slots), F32),
            pltpu.VMEM((PIECES, PLANES, 2 * slots, width), BF16),
            pltpu.VMEM((PIECES, 4, slots, width), BF16),
            pltpu.VMEM((PIECES, 4, slots, width), BF16),
            pltpu.VMEM((PLANES, DEPTH, width), F32),
            pltpu.VMEM((PIECES, 2 * DEPTH, width), F32),
            pltpu.VMEM((depth, points), F32),
            pltpu.VMEM((PIECES, 2, DEPTH, width), F32),
            pltpu.VMEM((PIECES, 2, DEPTH, width), F32),
            pltpu.VMEM((PIECES, DEPTH, width), F32),
            pltpu.VMEM((PIECES, DEPTH, width), F32),
            pltpu.VMEM((slots, 2 * slots), F32),
            pltpu.VMEM((2, slots, 2 * slots), F32),
            pltpu.VMEM((2, slots, 2 * slots), F32),
            pltpu.VMEM((slots, 3 * slots), F32),
            pltpu.VMEM((slots, 3 * slots), F32),
            pltpu.SemaphoreType.DMA((PIECES,)),
            pair,
            pair,
            pair,
            pair,
            pair,
            pltpu.SemaphoreType.DMA((2, 2)),
            pltpu.SemaphoreType.DMA((3,)),
        ],
        compiler_params=pltpu.CompilerParams(
            collective_id=0, has_side_effects=True, vmem_limit_bytes=56 * 2**20
        ),
        cost_estimate=pl.CostEstimate(
            flops=4 * 10**9, bytes_accessed=5 * 2**20, transcendentals=2**16
        ),
    )(
        basis_wavefunctions.reshape(slots * depth, points),
        filling_weights.reshape(1, slots),
        living_per_unit,
        starting_sheets.reshape(count, slots),
        nucleus_charge,
        applied_field,
    )
    return rho, ham, ovl


def solution(mesh):
    return jax.shard_map(
        per_device,
        mesh=mesh,
        in_specs=(P("func", None, None), P("func"), P(), P(), P("func", None), P("func", None)),
        out_specs=(P("func", None), P("func", None), P("func", None)),
        check_vma=False,
    )
```

profile of v0, /device:TPU:0, one launch (start us, length us, event | category | flops | bytes accessed | tf_op | source)
XLA Modules:
  0.0 50.6 jit_solution(1314094015720644690)
XLA Ops:
  0.6 45.2 %shard_map.85 = (f32[8,2048]{1,0:T(8,128)}, f32[128,384]{1,0:T(8,128)}, f32[128,384]{1,0:T(8,128)}) custom-call(bf16[1024,2048]{1,0:T(8,128)(2,1)} %bitcast.3, f32[1,128]{1,0:T(1,128)} %bitcast.5, s32[128]{0:T(128)} %living.1, s32[128,128]{1,0:T(8,128)} %bitcast.4, f32[8,2048]{1,0:T(8,128)} %nucleus.1, f32[8,2048]{1,0:T(8,128)} %applied.1), custom_call_target="tpu_custom_call" | custom-call | flops 4000000000 | bytes 5242880 | tf_op jit(solution)/shard_map/pallas_call | solution.py:309
  45.9 1.5 %copy.12 = f32[8,2048]{1,0:T(8,128)} copy(f32[8,2048]{1,0:T(8,128)} %get-tuple-element.6) | data formatting | bytes 131072
  47.4 1.6 %copy.13 = f32[128,384]{1,0:T(8,128)} copy(f32[128,384]{1,0:T(8,128)} %get-tuple-element.7) | data formatting | bytes 393216
  49.0 1.6 %copy.14 = f32[128,384]{1,0:T(8,128)} copy(f32[128,384]{1,0:T(8,128)} %get-tuple-element.8) | data formatting | bytes 393216
where the time goes:
time: 50.8 us; the launch traced here: 50.6 us
  Pallas kernels  45.2 us (89%)
  local copies, waits for them, and re-layouts  4.7 us (9%)
  between operations  0.64 us (1%)
    pallas_call x1, Pallas kernels, per_device(): pl.pallas_call(functools.partial(kernel, count), out_shape=(jax.ShapeDtyp...  45.2 us
    unnamed x3, local copies, waits for them, and re-layouts  4.7 us

commit v1 on v0

--- a/solution.py
+++ b/solution.py
@@ -17,6 +17,11 @@
 GROUP = 16
 GROUPS = SLOTS // GROUP
 PIECES = 4
+LEVELS = 4
+ROOM = (32, 64, 80, 96)
+FIRST = (0, 32, 96, 176)
+FEW, MANY = 176, 272
+PARTS = 96
 
 
 def dot_nt(a, b):
@@ -28,7 +33,365 @@
     return (2.0 * y + x / (y * y)) * (1.0 / 3.0)
 
 
-def kernel(
+def dot_nn(a, b):
+    return lax.dot_general(a, b, (((1,), (0,)), ((), ())), preferred_element_type=F32)
+
+
+def select_rows(one_hot, values):
+    high = values.astype(BF16)
+    low = (values - high.astype(F32)).astype(BF16)
+    return dot_nn(one_hot, high) + dot_nn(one_hot, low)
+
+
+def select_columns(values, one_hot):
+    high = values.astype(BF16)
+    low = (values - high.astype(F32)).astype(BF16)
+    return dot_nn(high, one_hot) + dot_nn(low, one_hot)
+
+
+def rank_matrix(key):
+    row = lax.broadcasted_iota(jnp.int32, (SLOTS, SLOTS), 0)
+    column = lax.broadcasted_iota(jnp.int32, (SLOTS, SLOTS), 1)
+    wide = jnp.broadcast_to(key, (SLOTS, SLOTS))
+    tall = wide.T
+    before = jnp.where((tall < wide) | ((tall == wide) & (row < column)), 1.0, 0.0)
+    rank = jnp.sum(before, axis=0, keepdims=True)
+    return jnp.where(row.astype(F32) == rank, 1.0, 0.0)
+
+
+def packed_kernel(
+    count,
+    boxes,
+    weights_in,
+    living_in,
+    sheets_in,
+    nucleus_in,
+    applied_in,
+    rho_out,
+    own_out,
+    side_out,
+    part_in,
+    back_out,
+    over_out,
+    raw,
+    weights,
+    living,
+    sheets,
+    nucleus,
+    applied,
+    starts,
+    selector,
+    wide_weights,
+    order,
+    back,
+    stack,
+    to_prev,
+    to_next,
+    from_prev,
+    from_next,
+    pot,
+    rho,
+    up_out,
+    up_in,
+    down_out,
+    down_in,
+    own,
+    part,
+    side,
+    raw_sem,
+    in_sems,
+    down_sems,
+    up_sems,
+    planes_down_sems,
+    planes_up_sems,
+    part_sems,
+    out_sems,
+):
+    me = lax.axis_index("func")
+    following = lax.rem(me + 1, count)
+    preceding = lax.rem(me + count - 1, count)
+    width = raw.shape[2]
+    step = min(width, 256)
+
+    def points(piece):
+        return pl.ds(pl.multiple_of(piece * width, width), width)
+
+    def raw_copy(piece):
+        return pltpu.make_async_copy(
+            boxes.at[:, points(piece)], raw.at[piece], raw_sem.at[piece]
+        )
+
+    small = [
+        pltpu.make_async_copy(source, target, in_sems.at[place])
+        for place, (source, target) in enumerate(
+            (
+                (sheets_in, sheets),
+                (living_in, living),
+                (weights_in, weights),
+                (nucleus_in, nucleus),
+                (applied_in, applied),
+            )
+        )
+    ]
+    for copy in small:
+        copy.start()
+    for piece in range(PIECES):
+        raw_copy(piece).start()
+
+    barrier = pltpu.get_barrier_semaphore()
+    for neighbour in (preceding, following):
+        pl.semaphore_signal(barrier, inc=1, device_id=(neighbour,), device_id_type=MESH)
+    for copy in small:
+        copy.wait()
+
+    alive = jnp.broadcast_to(living[...], (SLOTS, count)).T
+    lane = lax.broadcasted_iota(jnp.int32, (count, SLOTS), 1)
+    owner = lax.broadcasted_iota(jnp.int32, (count, SLOTS), 0)
+    starts[...] = jnp.where(lane < alive, sheets[...] - owner * DEPTH, 64).astype(F32)
+
+    start = starts[pl.ds(me, 1), :]
+    lanes = lax.broadcasted_iota(jnp.int32, (GROUPS, SLOTS), 1)
+    rows = lax.broadcasted_iota(jnp.int32, (GROUPS, SLOTS), 0)
+    spread = jnp.where(lanes // GROUP == rows, start, 0.0).astype(BF16)
+    repeat = (
+        lax.broadcasted_iota(jnp.int32, (SLOTS, SLOTS), 0) % GROUP
+        == lax.broadcasted_iota(jnp.int32, (SLOTS, SLOTS), 1) // DEPTH
+    )
+    column_start = dot_nn(spread, jnp.where(repeat, 1.0, 0.0).astype(BF16))
+    row = lax.broadcasted_iota(jnp.int32, (PLANES * GROUP, SLOTS), 0)
+    column = lax.broadcasted_iota(jnp.int32, (PLANES * GROUP, SLOTS), 1)
+    offset = jnp.where(
+        row % GROUP == column // DEPTH, row // GROUP - column % DEPTH, -99
+    ).astype(F32)
+    for group in range(GROUPS):
+        selector[group] = jnp.where(offset == column_start[group : group + 1, :], 1.0, 0.0).astype(BF16)
+    wide_weights[...] = jnp.broadcast_to(weights[...], (SLOTS, SLOTS)).T
+
+    def up_matrix(device):
+        return rank_matrix(starts[pl.ds(device, 1), :])
+
+    def down_matrix(device):
+        first = starts[pl.ds(device, 1), :]
+        return rank_matrix(jnp.where(first < 64.0, -first, first))
+
+    up_order = up_matrix(me)
+    down_order = down_matrix(me)
+    order[0] = up_order.astype(BF16)
+    order[1] = down_order.astype(BF16)
+    back[0] = up_order.T.astype(BF16)
+    back[1] = down_order.T.astype(BF16)
+
+    def down_copy(piece):
+        return pltpu.make_async_remote_copy(
+            src_ref=down_out.at[piece],
+            dst_ref=down_in.at[piece],
+            send_sem=down_sems.at[0, piece],
+            recv_sem=down_sems.at[1, piece],
+            device_id=(following,),
+            device_id_type=MESH,
+        )
+
+    def up_copy(piece):
+        return pltpu.make_async_remote_copy(
+            src_ref=up_out.at[piece],
+            dst_ref=up_in.at[piece],
+            send_sem=up_sems.at[0, piece],
+            recv_sem=up_sems.at[1, piece],
+            device_id=(preceding,),
+            device_id_type=MESH,
+        )
+
+    def planes_down_copy(piece, length):
+        return pltpu.make_async_remote_copy(
+            src_ref=to_next.at[piece, pl.ds(0, length)],
+            dst_ref=from_prev.at[piece, pl.ds(0, length)],
+            send_sem=planes_down_sems.at[0, piece],
+            recv_sem=planes_down_sems.at[1, piece],
+            device_id=(following,),
+            device_id_type=MESH,
+        )
+
+    def planes_up_copy(piece, length):
+        return pltpu.make_async_remote_copy(
+            src_ref=to_prev.at[piece, pl.ds(0, length)],
+            dst_ref=from_next.at[piece, pl.ds(0, length)],
+            send_sem=planes_up_sems.at[0, piece],
+            recv_sem=planes_up_sems.at[1, piece],
+            device_id=(preceding,),
+            device_id_type=MESH,
+        )
+
+    def place(piece):
+        raw_copy(piece).wait()
+        for part_of in range(width // step):
+            columns = pl.ds(part_of * step, step)
+            columns_of_all = pl.ds(pl.multiple_of(piece * width + part_of * step, step), step)
+            dens = jnp.zeros((PLANES, DEPTH, step), F32)
+            for group in range(GROUPS):
+                source = raw[piece, group * GROUP * DEPTH : (group + 1) * GROUP * DEPTH, columns]
+                placed = dot_nn(selector[group], source).reshape(PLANES, GROUP, step)
+                stack[piece, :, group * GROUP : (group + 1) * GROUP, columns] = placed.astype(BF16)
+                weight = wide_weights[group * GROUP : (group + 1) * GROUP, :]
+                weight = jnp.concatenate([weight] * (step // SLOTS), axis=1)
+                terms = placed * placed * weight[None]
+                dens += terms[:, :DEPTH] + terms[:, DEPTH:]
+            dens = jnp.sum(dens, axis=1)
+            down_out[piece, : DEPTH - 1, columns] = dens[DEPTH:]
+            down_out[piece, DEPTH - 1 :, columns] = jnp.zeros((1, step), F32)
+            up_out[piece, 0, :, columns] = nucleus[:, columns_of_all] + dens[:DEPTH]
+            up_out[piece, 1, :, columns] = applied[:, columns_of_all]
+
+    def pack_up(piece, level):
+        rows = pl.ds(FIRST[level], ROOM[level])
+        to_prev[piece, rows, :] = dot_nn(
+            order[0, : ROOM[level], :], stack[piece, level, :SLOTS, :]
+        ).astype(BF16)
+
+    def pack_down(piece, level):
+        rows = pl.ds(FIRST[level], ROOM[level])
+        to_next[piece, rows, :] = dot_nn(
+            order[1, : ROOM[level], :], stack[piece, 2 * DEPTH - 2 - level, :SLOTS, :]
+        ).astype(BF16)
+
+    def pack_and_send(piece):
+        down_copy(piece).start()
+        up_copy(piece).start()
+        for level in range(LEVELS - 1):
+            pack_up(piece, level)
+            pack_down(piece, level)
+
+        @pl.when(piece < PIECES // 2)
+        def _():
+            pack_up(piece, LEVELS - 1)
+            planes_up_copy(piece, MANY).start()
+            planes_down_copy(piece, FEW).start()
+
+        @pl.when(piece >= PIECES // 2)
+        def _():
+            pack_down(piece, LEVELS - 1)
+            planes_up_copy(piece, FEW).start()
+            planes_down_copy(piece, MANY).start()
+
+    place(0)
+    pl.semaphore_wait(barrier, 2)
+    pack_and_send(jnp.int32(0))
+
+    def place_piece(piece, carry):
+        place(piece)
+        pack_and_send(piece)
+        return carry
+
+    lax.fori_loop(1, PIECES, place_piece, 0)
+
+    over = jnp.zeros((count, 1), F32)
+    first = starts[...]
+    for level in range(LEVELS):
+        low = jnp.sum(jnp.where(first <= level, 1.0, 0.0), axis=1, keepdims=True)
+        high = jnp.sum(
+            jnp.where((first >= DEPTH - 1 - level) & (first < 64.0), 1.0, 0.0), axis=1, keepdims=True
+        )
+        over = jnp.maximum(over, jnp.maximum(low, high) - ROOM[level])
+    over_out[0] = jnp.max(over)
+
+    own[...] = jnp.zeros_like(own)
+
+    def own_piece(piece, carry):
+        down_copy(piece).wait()
+        up_copy(piece).wait()
+        density = up_out[piece, 0] + down_in[piece]
+        rho[:, points(piece)] = density
+        pot[piece, :DEPTH] = up_out[piece, 1] - 0.9847 * cube_root(density)
+        pot[piece, DEPTH:] = up_in[piece, 1] - 0.9847 * cube_root(up_in[piece, 0] + down_out[piece])
+        total = own[...]
+        for plane in range(PLANES):
+            phi = stack[piece, plane, :SLOTS, :]
+            stack[piece, plane, SLOTS:, :] = (phi.astype(F32) * pot[piece, plane : plane + 1, :]).astype(BF16)
+            total += dot_nt(phi, stack[piece, plane])
+        own[...] = total
+        return carry
+
+    lax.fori_loop(0, PIECES, own_piece, 0)
+    rho_copy = pltpu.make_async_copy(rho, rho_out, out_sems.at[0])
+    own_copy = pltpu.make_async_copy(own, own_out, out_sems.at[1])
+    back_copy = pltpu.make_async_copy(back, back_out, out_sems.at[2])
+    rho_copy.start()
+    own_copy.start()
+    back_copy.start()
+
+    part[...] = jnp.zeros_like(part)
+
+    def cross_next(piece, level):
+        part[0, : ROOM[level], :] += dot_nt(
+            from_next[piece, FIRST[level] : FIRST[level] + ROOM[level], :],
+            stack[piece, DEPTH + level],
+        )
+
+    def cross_prev(piece, level):
+        part[1, : ROOM[level], :] += dot_nt(
+            from_prev[piece, FIRST[level] : FIRST[level] + ROOM[level], :],
+            stack[piece, DEPTH - 2 - level],
+        )
+
+    def cross_piece(piece, carry):
+        @pl.when(piece < PIECES // 2)
+        def _():
+            planes_up_copy(piece, MANY).wait()
+            planes_down_copy(piece, FEW).wait()
+            cross_next(piece, LEVELS - 1)
+
+        @pl.when(piece >= PIECES // 2)
+        def _():
+            planes_up_copy(piece, FEW).wait()
+            planes_down_copy(piece, MANY).wait()
+            cross_prev(piece, LEVELS - 1)
+
+        for level in range(LEVELS - 1):
+            cross_next(piece, level)
+            cross_prev(piece, level)
+        return carry
+
+    lax.fori_loop(0, PIECES, cross_piece, 0)
+
+    def part_copy(which, target):
+        return pltpu.make_async_remote_copy(
+            src_ref=part.at[which, pl.ds(0, PARTS)],
+            dst_ref=part_in.at[which],
+            send_sem=part_sems.at[0, which],
+            recv_sem=part_sems.at[1, which],
+            device_id=(target,),
+            device_id_type=MESH,
+        )
+
+    part_to_next = part_copy(0, following)
+    part_to_prev = part_copy(1, preceding)
+    part_to_next.start()
+    part_to_prev.start()
+    side[0] = select_columns(part[0].T, up_matrix(following).astype(BF16))
+    side[1] = select_columns(part[1].T, down_matrix(preceding).astype(BF16))
+    side_copy = pltpu.make_async_copy(side, side_out, out_sems.at[3])
+    side_copy.start()
+    rho_copy.wait()
+    own_copy.wait()
+    back_copy.wait()
+    side_copy.wait()
+    part_to_next.wait()
+    part_to_prev.wait()
+
+
+def finish_kernel(scale, rho, own, side, part_in, back, rho_out, ham_out, ovl_out):
+    rho_out[...] = rho[...]
+    none = jnp.zeros((SLOTS - PARTS, 2 * SLOTS), F32)
+    from_prev = select_rows(back[0], jnp.concatenate([part_in[0], none], axis=0))
+    from_next = select_rows(back[1], jnp.concatenate([part_in[1], none], axis=0))
+    ovl_out[:, :SLOTS] = (side[1, :SLOTS, :] + from_prev[:, :SLOTS]) * scale
+    ham_out[:, :SLOTS] = (side[1, SLOTS:, :] + from_prev[:, SLOTS:]) * scale
+    ovl_out[:, SLOTS : 2 * SLOTS] = own[:, :SLOTS] * scale
+    ham_out[:, SLOTS : 2 * SLOTS] = own[:, SLOTS:] * scale
+    ovl_out[:, 2 * SLOTS :] = (side[0, :SLOTS, :] + from_next[:, :SLOTS]) * scale
+    ham_out[:, 2 * SLOTS :] = (side[0, SLOTS:, :] + from_next[:, SLOTS:]) * scale
+
+
+def full_kernel(
     count,
     boxes,
     weights,
@@ -292,7 +655,7 @@
     ham_copy.wait()
 
 
-def per_device(
+def full_call(
     basis_wavefunctions,
     filling_weights,
     living_per_unit,
@@ -306,8 +669,8 @@
     vmem = pl.BlockSpec(memory_space=pltpu.VMEM)
     anywhere = pl.BlockSpec(memory_space=pl.ANY)
     pair = pltpu.SemaphoreType.DMA((2, PIECES))
-    rho, ham, ovl = pl.pallas_call(
-        functools.partial(kernel, count),
+    return pl.pallas_call(
+        functools.partial(full_kernel, count),
         out_shape=(
             jax.ShapeDtypeStruct((depth, points), F32),
             jax.ShapeDtypeStruct((slots, 3 * slots), F32),
@@ -351,7 +714,7 @@
             pltpu.SemaphoreType.DMA((3,)),
         ],
         compiler_params=pltpu.CompilerParams(
-            collective_id=0, has_side_effects=True, vmem_limit_bytes=56 * 2**20
+            collective_id=1, has_side_effects=True, vmem_limit_bytes=56 * 2**20
         ),
         cost_estimate=pl.CostEstimate(
             flops=4 * 10**9, bytes_accessed=5 * 2**20, transcendentals=2**16
@@ -364,7 +727,108 @@
         nucleus_charge,
         applied_field,
     )
-    return rho, ham, ovl
+
+
+def per_device(
+    basis_wavefunctions,
+    filling_weights,
+    living_per_unit,
+    starting_sheets,
+    nucleus_charge,
+    applied_field,
+):
+    slots, depth, points = basis_wavefunctions.shape
+    count = lax.axis_size("func")
+    width = points // PIECES
+    anywhere = pl.BlockSpec(memory_space=pl.ANY)
+    pair = pltpu.SemaphoreType.DMA((2, PIECES))
+    rho, own, side, part_in, back, over = pl.pallas_call(
+        functools.partial(packed_kernel, count),
+        out_shape=(
+            jax.ShapeDtypeStruct((depth, points), F32),
+            jax.ShapeDtypeStruct((slots, 2 * slots), F32),
+            jax.ShapeDtypeStruct((2, 2 * slots, slots), F32),
+            jax.ShapeDtypeStruct((2, PARTS, 2 * slots), F32),
+            jax.ShapeDtypeStruct((2, slots, slots), BF16),
+            jax.ShapeDtypeStruct((1,), F32),
+        ),
+        in_specs=[anywhere] * 6,
+        out_specs=(anywhere,) * 5 + (pl.BlockSpec(memory_space=pltpu.SMEM),),
+        scratch_shapes=[
+            pltpu.VMEM((PIECES, slots * depth, width), BF16),
+            pltpu.VMEM((1, slots), F32),
+            pltpu.VMEM((1, count), jnp.int32),
+            pltpu.VMEM((count, slots), jnp.int32),
+            pltpu.VMEM((depth, points), F32),
+            pltpu.VMEM((depth, points), F32),
+            pltpu.VMEM((count, slots), F32),
+            pltpu.VMEM((GROUPS, PLANES * GROUP, slots), BF16),
+            pltpu.VMEM((slots, slots), F32),
+            pltpu.VMEM((2, slots, slots), BF16),
+            pltpu.VMEM((2, slots, slots), BF16),
+            pltpu.VMEM((PIECES, PLANES, 2 * slots, width), BF16),
+            pltpu.VMEM((PIECES, MANY, width), BF16),
+            pltpu.VMEM((PIECES, MANY, width), BF16),
+            pltpu.VMEM((PIECES, MANY, width), BF16),
+            pltpu.VMEM((PIECES, MANY, width), BF16),
+            pltpu.VMEM((PIECES, 2 * DEPTH, width), F32),
+            pltpu.VMEM((depth, points), F32),
+            pltpu.VMEM((PIECES, 2, DEPTH, width), F32),
+            pltpu.VMEM((PIECES, 2, DEPTH, width), F32),
+            pltpu.VMEM((PIECES, DEPTH, width), F32),
+            pltpu.VMEM((PIECES, DEPTH, width), F32),
+            pltpu.VMEM((slots, 2 * slots), F32),
+            pltpu.VMEM((2, slots, 2 * slots), F32),
+            pltpu.VMEM((2, 2 * slots, slots), F32),
+            pltpu.SemaphoreType.DMA((PIECES,)),
+            pltpu.SemaphoreType.DMA((5,)),
+            pair,
+            pair,
+            pair,
+            pair,
+            pltpu.SemaphoreType.DMA((2, 2)),
+            pltpu.SemaphoreType.DMA((4,)),
+        ],
+        compiler_params=pltpu.CompilerParams(
+            collective_id=0, has_side_effects=True, vmem_limit_bytes=56 * 2**20
+        ),
+        cost_estimate=pl.CostEstimate(
+            flops=4 * 10**9, bytes_accessed=5 * 2**20, transcendentals=2**16
+        ),
+    )(
+        basis_wavefunctions.reshape(slots * depth, points),
+        filling_weights.reshape(1, slots),
+        living_per_unit.reshape(1, count),
+        starting_sheets.reshape(count, slots),
+        nucleus_charge,
+        applied_field,
+    )
+
+    def finish():
+        return tuple(
+            pl.pallas_call(
+                functools.partial(finish_kernel, 1.0 / (depth * points)),
+                out_shape=(
+                    jax.ShapeDtypeStruct((depth, points), F32),
+                    jax.ShapeDtypeStruct((slots, 3 * slots), F32),
+                    jax.ShapeDtypeStruct((slots, 3 * slots), F32),
+                ),
+            )(rho, own, side, part_in, back)
+        )
+
+    def in_full():
+        return tuple(
+            full_call(
+                basis_wavefunctions,
+                filling_weights,
+                living_per_unit,
+                starting_sheets,
+                nucleus_charge,
+                applied_field,
+            )
+        )
+
+    return lax.cond(over[0] > 0.0, in_full, finish)
 
 
 def solution(mesh):

time: 50.8 us -> 38.1 us (0.75)
  Pallas kernels: 45.2 us -> 34.6 us
  local copies, waits for them, and re-layouts: 4.7 us -> 2.01 us
  between operations: 0.64 us -> 1.35 us
    pallas_call x1 -> x2, Pallas kernels: 45.2 us -> 34.6 us  [the longest x1 34.3 us: per_device(): pl.pallas_call(functools.partial(packed_kernel, count), out_shape=(jax.Sh...]
    unnamed x3 -> x13, local copies, waits for them, and re-layouts: 4.7 us -> 2.01 us
where the time goes in v1:
time: 38.1 us; the launch traced here: 38 us
  Pallas kernels  34.6 us (91%)
  local copies, waits for them, and re-layouts  2.01 us (5%)
  between operations  1.35 us (4%)
    pallas_call x1, Pallas kernels, per_device(): pl.pallas_call(functools.partial(packed_kernel, count), out_shape=(jax.Sh...  34.3 us
    unnamed x13, local copies, waits for them, and re-layouts  2.01 us

profile of v1, /device:TPU:0, one launch (start us, length us, event | category | flops | bytes accessed | tf_op | source)
XLA Modules:
  0.0 38.0 jit_solution(7294021030935601990)
XLA Ops:
  0.6 0.0 copy-start
  0.6 0.0 copy-start.1
  0.7 0.0 copy-start.2
  0.7 0.0 copy-start.3
  0.7 0.0 copy-start.4
  0.7 34.3 %shard_map.91 = (f32[8,2048]{1,0:T(8,128)S(1)}, f32[128,256]{1,0:T(8,128)S(1)}, f32[2,256,128]{2,1,0:T(8,128)S(1)}, f32[2,96,256]{2,1,0:T(8,128)S(1)}, bf16[2,128,128]{2,1,0:T(8,128)(2,1)S(1)}, /*index=5*/f32[1]{0:T(128)}) custom-call(bf16[1024,2048]{1,0:T(8,128)(2,1)} %bitcast.8, f32[1,128]{1,0:T(1,128)} %bitcast.12, s32[1,128]{1,0:T(1,128)} %bitcast.14, ...), custom_call_target="tpu_custom_call" | custom-call | flops 4000000000 | bytes 5242880 | tf_op jit(solution)/shard_map/pallas_call | solution.py:745
  35.7 0.0 copy-done
  35.7 0.0 copy-done.1
  35.7 0.0 copy-done.2
  35.7 0.0 copy-done.3
  35.7 0.0 copy-done.4
  35.7 0.3 conditional.1
  35.7 0.2 branch_0_fun.1
  36.0 0.6 %copy.24 = f32[8,2048]{1,0:T(8,128)} copy(f32[8,2048]{1,0:T(8,128)S(1)} %get-tuple-element.66) | data formatting | bytes 131072
  36.6 0.7 %copy.25 = f32[128,384]{1,0:T(8,128)} copy(f32[128,384]{1,0:T(8,128)S(1)} %get-tuple-element.67) | data formatting | bytes 393216
  37.3 0.7 %copy.26 = f32[128,384]{1,0:T(8,128)} copy(f32[128,384]{1,0:T(8,128)S(1)} %get-tuple-element.68) | data formatting | bytes 393216
Async XLA Ops:
  0.6 35.0 %copy-start = (s32[16384]{0:T(1024)S(1)}, s32[16384]{0:T(1024)}, u32[]{:S(2)}) copy-start(s32[16384]{0:T(1024)} %param.11) | copy-start | bytes 196612
  0.6 35.0 %copy-start.1 = (f32[8,2048]{1,0:T(8,128)S(1)}, f32[8,2048]{1,0:T(8,128)}, u32[]{:S(2)}) copy-start(f32[8,2048]{1,0:T(8,128)} %nucleus_in.1) | copy-start | bytes 196612
  0.7 35.0 %copy-start.2 = (f32[8,2048]{1,0:T(8,128)S(1)}, f32[8,2048]{1,0:T(8,128)}, u32[]{:S(2)}) copy-start(f32[8,2048]{1,0:T(8,128)} %applied_in.1) | copy-start | bytes 196612
  0.7 35.0 %copy-start.3 = (f32[128]{0:T(128)S(1)}, f32[128]{0:T(128)}, u32[]{:S(2)}) copy-start(f32[128]{0:T(128)} %param.9) | copy-start | bytes 1540
  0.7 35.0 %copy-start.4 = (s32[128]{0:T(128)S(1)}, s32[128]{0:T(128)}, u32[]{:S(2)}) copy-start(s32[128]{0:T(128)} %param.10) | copy-start | bytes 1540

commit v2 on v1

--- a/solution.py
+++ b/solution.py
@@ -22,6 +22,8 @@
 FIRST = (0, 32, 96, 176)
 FEW, MANY = 176, 272
 PARTS = 96
+LAYERS = 4
+UP_PIECES = 1
 
 
 def dot_nt(a, b):
@@ -91,6 +93,7 @@
     from_next,
     pot,
     rho,
+    base,
     up_out,
     up_in,
     down_out,
@@ -238,8 +241,10 @@
             dens = jnp.sum(dens, axis=1)
             down_out[piece, : DEPTH - 1, columns] = dens[DEPTH:]
             down_out[piece, DEPTH - 1 :, columns] = jnp.zeros((1, step), F32)
-            up_out[piece, 0, :, columns] = nucleus[:, columns_of_all] + dens[:DEPTH]
-            up_out[piece, 1, :, columns] = applied[:, columns_of_all]
+            below = nucleus[:, columns_of_all] + dens[:DEPTH]
+            base[piece, :, columns] = below
+            up_out[piece, :DEPTH, columns] = below.astype(BF16)
+            up_out[piece, DEPTH:, columns] = applied[:, columns_of_all].astype(BF16)
 
     def pack_up(piece, level):
         rows = pl.ds(FIRST[level], ROOM[level])
@@ -253,35 +258,67 @@
             order[1, : ROOM[level], :], stack[piece, 2 * DEPTH - 2 - level, :SLOTS, :]
         ).astype(BF16)
 
-    def pack_and_send(piece):
-        down_copy(piece).start()
-        up_copy(piece).start()
+    def pack(piece):
         for level in range(LEVELS - 1):
             pack_up(piece, level)
             pack_down(piece, level)
 
-        @pl.when(piece < PIECES // 2)
+        @pl.when(piece < UP_PIECES)
         def _():
             pack_up(piece, LEVELS - 1)
+
+        @pl.when(piece >= UP_PIECES)
+        def _():
+            pack_down(piece, LEVELS - 1)
+
+    def send_density(piece):
+        down_copy(piece).start()
+        up_copy(piece).start()
+
+    def send_planes(piece):
+        @pl.when(piece < UP_PIECES)
+        def _():
             planes_up_copy(piece, MANY).start()
             planes_down_copy(piece, FEW).start()
 
-        @pl.when(piece >= PIECES // 2)
-        def _():
-            pack_down(piece, LEVELS - 1)
+        @pl.when(piece >= UP_PIECES)
+        def _():
             planes_up_copy(piece, FEW).start()
             planes_down_copy(piece, MANY).start()
 
-    place(0)
+    def place_and_pack(piece, carry):
+        place(piece)
+        pack(piece)
+        return carry
+
+    late = lax.rem(me, max(count // LAYERS, 1)) == 0
+    place_and_pack(jnp.int32(0), 0)
+
+    @pl.when(late)
+    def _():
+        lax.fori_loop(1, PIECES, place_and_pack, 0)
+
     pl.semaphore_wait(barrier, 2)
-    pack_and_send(jnp.int32(0))
-
-    def place_piece(piece, carry):
-        place(piece)
-        pack_and_send(piece)
+    send_density(jnp.int32(0))
+
+    @pl.when(late)
+    def _():
+        for piece in range(1, PIECES):
+            send_density(piece)
+
+    send_planes(jnp.int32(0))
+
+    def next_piece(piece, carry):
+        @pl.when(jnp.logical_not(late))
+        def _():
+            place(piece)
+            send_density(piece)
+            pack(piece)
+
+        send_planes(piece)
         return carry
 
-    lax.fori_loop(1, PIECES, place_piece, 0)
+    lax.fori_loop(1, PIECES, next_piece, 0)
 
     over = jnp.zeros((count, 1), F32)
     first = starts[...]
@@ -298,10 +335,11 @@
     def own_piece(piece, carry):
         down_copy(piece).wait()
         up_copy(piece).wait()
-        density = up_out[piece, 0] + down_in[piece]
+        density = base[piece] + down_in[piece]
         rho[:, points(piece)] = density
-        pot[piece, :DEPTH] = up_out[piece, 1] - 0.9847 * cube_root(density)
-        pot[piece, DEPTH:] = up_in[piece, 1] - 0.9847 * cube_root(up_in[piece, 0] + down_out[piece])
+        pot[piece, :DEPTH] = applied[:, points(piece)] - 0.9847 * cube_root(density)
+        above = up_in[piece].astype(F32)
+        pot[piece, DEPTH:] = above[DEPTH:] - 0.9847 * cube_root(above[:DEPTH] + down_out[piece])
         total = own[...]
         for plane in range(PLANES):
             phi = stack[piece, plane, :SLOTS, :]
@@ -333,13 +371,13 @@
         )
 
     def cross_piece(piece, carry):
-        @pl.when(piece < PIECES // 2)
+        @pl.when(piece < UP_PIECES)
         def _():
             planes_up_copy(piece, MANY).wait()
             planes_down_copy(piece, FEW).wait()
             cross_next(piece, LEVELS - 1)
 
-        @pl.when(piece >= PIECES // 2)
+        @pl.when(piece >= UP_PIECES)
         def _():
             planes_up_copy(piece, FEW).wait()
             planes_down_copy(piece, MANY).wait()
@@ -399,9 +437,7 @@
     sheets,
     nucleus,
     applied,
-    rho_out,
-    ham_out,
-    ovl_out,
+    side_out,
     raw,
     selector,
     wide_weights,
@@ -410,16 +446,13 @@
     from_next,
     dens,
     pot,
-    rho,
     up_out,
     up_in,
     down_out,
     down_in,
-    own,
     part,
     part_in,
-    ham,
-    ovl,
+    side,
     raw_sem,
     down_sems,
     up_sems,
@@ -427,7 +460,7 @@
     planes_up_sems,
     plane_sems,
     part_sems,
-    out_sems,
+    out_sem,
 ):
     me = lax.axis_index("func")
     following = lax.rem(me + 1, count)
@@ -570,28 +603,18 @@
 
     lax.fori_loop(0, PIECES, place_piece, 0)
 
-    own[...] = jnp.zeros_like(own)
-
     def own_piece(piece, carry):
         down_copy(piece).wait()
         up_copy(piece).wait()
         density = up_out[piece, 0] + down_in[piece]
-        rho[:, points(piece)] = density
         pot[piece, :DEPTH] = up_out[piece, 1] - 0.9847 * cube_root(density)
         pot[piece, DEPTH:] = up_in[piece, 1] - 0.9847 * cube_root(up_in[piece, 0] + down_out[piece])
-        total = own[...]
         for plane in range(PLANES):
             phi = stack[piece, plane, :SLOTS, :]
             stack[piece, plane, SLOTS:, :] = (phi.astype(F32) * pot[piece, plane : plane + 1, :]).astype(BF16)
-            total += dot_nt(phi, stack[piece, plane])
-        own[...] = total
         return carry
 
     lax.fori_loop(0, PIECES, own_piece, 0)
-    rho_copy = pltpu.make_async_copy(rho, rho_out, out_sems.at[0])
-    rho_copy.start()
-
-    scale = 1.0 / (DEPTH * width * PIECES)
     part[...] = jnp.zeros_like(part)
 
     def cross_piece(piece, carry):
@@ -634,25 +657,15 @@
     to_prev = part_copy(1, preceding)
     to_next.start()
     to_prev.start()
-    ovl[:, SLOTS : 2 * SLOTS] = own[:, :SLOTS] * scale
-    ham[:, SLOTS : 2 * SLOTS] = own[:, SLOTS:] * scale
-    ovl_next = part[0, :, :SLOTS].T
-    ham_next = part[0, :, SLOTS:].T
-    ovl_prev = part[1, :, :SLOTS].T
-    ham_prev = part[1, :, SLOTS:].T
     to_next.wait()
     to_prev.wait()
-    ovl[:, :SLOTS] = (ovl_prev + part_in[0, :, :SLOTS]) * scale
-    ham[:, :SLOTS] = (ham_prev + part_in[0, :, SLOTS:]) * scale
-    ovl[:, 2 * SLOTS :] = (ovl_next + part_in[1, :, :SLOTS]) * scale
-    ham[:, 2 * SLOTS :] = (ham_next + part_in[1, :, SLOTS:]) * scale
-    ovl_copy = pltpu.make_async_copy(ovl, ovl_out, out_sems.at[1])
-    ham_copy = pltpu.make_async_copy(ham, ham_out, out_sems.at[2])
-    ovl_copy.start()
-    ham_copy.start()
-    rho_copy.wait()
-    ovl_copy.wait()
-    ham_copy.wait()
+    side[0, :SLOTS] = part[0, :, :SLOTS].T + part_in[1, :, :SLOTS]
+    side[0, SLOTS:] = part[0, :, SLOTS:].T + part_in[1, :, SLOTS:]
+    side[1, :SLOTS] = part[1, :, :SLOTS].T + part_in[0, :, :SLOTS]
+    side[1, SLOTS:] = part[1, :, SLOTS:].T + part_in[0, :, SLOTS:]
+    side_copy = pltpu.make_async_copy(side, side_out, out_sem)
+    side_copy.start()
+    side_copy.wait()
 
 
 def full_call(
@@ -671,11 +684,7 @@
     pair = pltpu.SemaphoreType.DMA((2, PIECES))
     return pl.pallas_call(
         functools.partial(full_kernel, count),
-        out_shape=(
-            jax.ShapeDtypeStruct((depth, points), F32),
-            jax.ShapeDtypeStruct((slots, 3 * slots), F32),
-            jax.ShapeDtypeStruct((slots, 3 * slots), F32),
-        ),
+        out_shape=jax.ShapeDtypeStruct((2, 2 * slots, slots), F32),
         in_specs=[
             anywhere,
             vmem,
@@ -684,7 +693,7 @@
             vmem,
             vmem,
         ],
-        out_specs=(anywhere, anywhere, anywhere),
+        out_specs=anywhere,
         scratch_shapes=[
             pltpu.VMEM((PIECES, slots * depth, width), BF16),
             pltpu.VMEM((GROUPS, PLANES * GROUP, slots), BF16),
@@ -694,16 +703,13 @@
             pltpu.VMEM((PIECES, 4, slots, width), BF16),
             pltpu.VMEM((PLANES, DEPTH, width), F32),
             pltpu.VMEM((PIECES, 2 * DEPTH, width), F32),
-            pltpu.VMEM((depth, points), F32),
             pltpu.VMEM((PIECES, 2, DEPTH, width), F32),
             pltpu.VMEM((PIECES, 2, DEPTH, width), F32),
             pltpu.VMEM((PIECES, DEPTH, width), F32),
             pltpu.VMEM((PIECES, DEPTH, width), F32),
-            pltpu.VMEM((slots, 2 * slots), F32),
             pltpu.VMEM((2, slots, 2 * slots), F32),
             pltpu.VMEM((2, slots, 2 * slots), F32),
-            pltpu.VMEM((slots, 3 * slots), F32),
-            pltpu.VMEM((slots, 3 * slots), F32),
+            pltpu.VMEM((2, 2 * slots, slots), F32),
             pltpu.SemaphoreType.DMA((PIECES,)),
             pair,
             pair,
@@ -711,7 +717,7 @@
             pair,
             pair,
             pltpu.SemaphoreType.DMA((2, 2)),
-            pltpu.SemaphoreType.DMA((3,)),
+            pltpu.SemaphoreType.DMA,
         ],
         compiler_params=pltpu.CompilerParams(
             collective_id=1, has_side_effects=True, vmem_limit_bytes=56 * 2**20
@@ -773,8 +779,9 @@
             pltpu.VMEM((PIECES, MANY, width), BF16),
             pltpu.VMEM((PIECES, 2 * DEPTH, width), F32),
             pltpu.VMEM((depth, points), F32),
-            pltpu.VMEM((PIECES, 2, DEPTH, width), F32),
-            pltpu.VMEM((PIECES, 2, DEPTH, width), F32),
+            pltpu.VMEM((PIECES, DEPTH, width), F32),
+            pltpu.VMEM((PIECES, 2 * DEPTH, width), BF16),
+            pltpu.VMEM((PIECES, 2 * DEPTH, width), BF16),
             pltpu.VMEM((PIECES, DEPTH, width), F32),
             pltpu.VMEM((PIECES, DEPTH, width), F32),
             pltpu.VMEM((slots, 2 * slots), F32),
@@ -804,31 +811,31 @@
         applied_field,
     )
 
-    def finish():
-        return tuple(
-            pl.pallas_call(
-                functools.partial(finish_kernel, 1.0 / (depth * points)),
-                out_shape=(
-                    jax.ShapeDtypeStruct((depth, points), F32),
-                    jax.ShapeDtypeStruct((slots, 3 * slots), F32),
-                    jax.ShapeDtypeStruct((slots, 3 * slots), F32),
-                ),
-            )(rho, own, side, part_in, back)
-        )
+    def as_sent():
+        return side, part_in
 
     def in_full():
-        return tuple(
-            full_call(
-                basis_wavefunctions,
-                filling_weights,
-                living_per_unit,
-                starting_sheets,
-                nucleus_charge,
-                applied_field,
-            )
-        )
-
-    return lax.cond(over[0] > 0.0, in_full, finish)
+        whole = full_call(
+            basis_wavefunctions,
+            filling_weights,
+            living_per_unit,
+            starting_sheets,
+            nucleus_charge,
+            applied_field,
+        )
+        return whole, jnp.zeros_like(part_in)
+
+    side_blocks, received = lax.cond(over[0] > 0.0, in_full, as_sent)
+    return tuple(
+        pl.pallas_call(
+            functools.partial(finish_kernel, 1.0 / (depth * points)),
+            out_shape=(
+                jax.ShapeDtypeStruct((depth, points), F32),
+                jax.ShapeDtypeStruct((slots, 3 * slots), F32),
+                jax.ShapeDtypeStruct((slots, 3 * slots), F32),
+            ),
+        )(rho, own, side_blocks, received, back)
+    )
 
 
 def solution(mesh):

time: 38.1 us -> 33.7 us (0.88)
  Pallas kernels: 34.6 us -> 32.2 us
  local copies, waits for them, and re-layouts: 2.01 us -> 0.02 us
    pallas_call x1, Pallas kernels: 34.3 us -> 30.3 us  [per_device(): pl.pallas_call(functools.partial(packed_kernel, count), out_shape=(jax.Sh...]
    unnamed x13 -> x10, local copies, waits for them, and re-layouts: 2.01 us -> 0.02 us
    pallas_call x1, Pallas kernels: 0.23 us -> 1.91 us  [per_device(): pl.pallas_call(functools.partial(finish_kernel, 1.0 / (depth * points)),...]
where the time goes in v2:
time: 33.7 us; the launch traced here: 33.6 us
  Pallas kernels  32.2 us (96%)
  between operations  1.35 us (4%)
    pallas_call x1, Pallas kernels, per_device(): pl.pallas_call(functools.partial(packed_kernel, count), out_shape=(jax.Sh...  30.3 us
    pallas_call x1, Pallas kernels, per_device(): pl.pallas_call(functools.partial(finish_kernel, 1.0 / (depth * points)),...  1.91 us

profile of v2, /device:TPU:0, one launch (start us, length us, event | category | flops | bytes accessed | tf_op | source)
XLA Modules:
  0.0 33.6 jit_solution(12617087764990436166)
XLA Ops:
  0.6 0.0 copy-start
  0.6 0.0 copy-start.1
  0.7 0.0 copy-start.2
  0.7 0.0 copy-start.3
  0.7 0.0 copy-start.4
  0.7 30.3 %shard_map.85 = (f32[8,2048]{1,0:T(8,128)}, f32[128,256]{1,0:T(8,128)}, f32[2,256,128]{2,1,0:T(8,128)S(1)}, f32[2,96,256]{2,1,0:T(8,128)S(1)}, bf16[2,128,128]{2,1,0:T(8,128)(2,1)}, /*index=5*/f32[1]{0:T(128)}) custom-call(bf16[1024,2048]{1,0:T(8,128)(2,1)} %bitcast.8, f32[1,128]{1,0:T(1,128)} %bitcast.12, s32[1,128]{1,0:T(1,128)} %bitcast.14, ...), custom_call_target="tpu_custom_call" | custom-call | flops 4000000000 | bytes 5242880 | tf_op jit(solution)/shard_map/pallas_call | solution.py:751
  31.6 0.0 copy-done
  31.6 0.0 copy-done.1
  31.6 0.0 copy-done.2
  31.6 0.0 copy-done.3
  31.6 0.0 copy-done.4
  31.6 1.9 %shard_map.86 = (f32[8,2048]{1,0:T(8,128)}, f32[128,384]{1,0:T(8,128)}, f32[128,384]{1,0:T(8,128)}) custom-call(f32[8,2048]{1,0:T(8,128)} %get-tuple-element.33.rho, f32[128,256]{1,0:T(8,128)} %get-tuple-element.34.own, f32[2,256,128]{2,1,0:T(8,128)S(1)} %get-tuple-element.38.side, f32[2,96,256]{2,1,0:T(8,128)S(1)} %get-tuple-element.39.part_in, ...), custom_call_target="tpu_custom_call" | custom-call | tf_op jit(solution)/shard_map/pallas_call | solution.py:830
  (1 shorter events, 0.0 us)
Async XLA Ops:
  0.6 31.0 %copy-start = (s32[16384]{0:T(1024)S(1)}, s32[16384]{0:T(1024)}, u32[]{:S(2)}) copy-start(s32[16384]{0:T(1024)} %param.11) | copy-start | bytes 196612
  0.6 31.0 %copy-start.1 = (f32[8,2048]{1,0:T(8,128)S(1)}, f32[8,2048]{1,0:T(8,128)}, u32[]{:S(2)}) copy-start(f32[8,2048]{1,0:T(8,128)} %nucleus_in.1) | copy-start | bytes 196612
  0.7 31.0 %copy-start.2 = (f32[8,2048]{1,0:T(8,128)S(1)}, f32[8,2048]{1,0:T(8,128)}, u32[]{:S(2)}) copy-start(f32[8,2048]{1,0:T(8,128)} %applied_in.1) | copy-start | bytes 196612
  0.7 31.0 %copy-start.3 = (f32[128]{0:T(128)S(1)}, f32[128]{0:T(128)}, u32[]{:S(2)}) copy-start(f32[128]{0:T(128)} %param.9) | copy-start | bytes 1540
  0.7 31.0 %copy-start.4 = (s32[128]{0:T(128)S(1)}, s32[128]{0:T(128)}, u32[]{:S(2)}) copy-start(s32[128]{0:T(128)} %param.10) | copy-start | bytes 1540

commit v3 on v2

--- a/solution.py
+++ b/solution.py
@@ -332,23 +332,35 @@
 
     own[...] = jnp.zeros_like(own)
 
-    def own_piece(piece, carry):
-        down_copy(piece).wait()
-        up_copy(piece).wait()
+    def own_planes(piece, planes):
+        overlap = own[:, :SLOTS]
+        energy = own[:, SLOTS:]
+        for plane in planes:
+            phi = stack[piece, plane, :SLOTS, :]
+            vphi = (phi.astype(F32) * pot[piece, plane : plane + 1, :]).astype(BF16)
+            stack[piece, plane, SLOTS:, :] = vphi
+            overlap += dot_nt(phi, phi)
+            energy += dot_nt(phi, vphi)
+        own[:, :SLOTS] = overlap
+        own[:, SLOTS:] = energy
+
+    def low_planes(piece, carry):
+        down_copy(piece).wait_recv()
         density = base[piece] + down_in[piece]
         rho[:, points(piece)] = density
         pot[piece, :DEPTH] = applied[:, points(piece)] - 0.9847 * cube_root(density)
+        own_planes(piece, range(DEPTH))
+        return carry
+
+    def high_planes(piece, carry):
+        up_copy(piece).wait_recv()
         above = up_in[piece].astype(F32)
         pot[piece, DEPTH:] = above[DEPTH:] - 0.9847 * cube_root(above[:DEPTH] + down_out[piece])
-        total = own[...]
-        for plane in range(PLANES):
-            phi = stack[piece, plane, :SLOTS, :]
-            stack[piece, plane, SLOTS:, :] = (phi.astype(F32) * pot[piece, plane : plane + 1, :]).astype(BF16)
-            total += dot_nt(phi, stack[piece, plane])
-        own[...] = total
+        own_planes(piece, range(DEPTH, PLANES))
         return carry
 
-    lax.fori_loop(0, PIECES, own_piece, 0)
+    lax.fori_loop(0, PIECES, low_planes, 0)
+    lax.fori_loop(0, PIECES, high_planes, 0)
     rho_copy = pltpu.make_async_copy(rho, rho_out, out_sems.at[0])
     own_copy = pltpu.make_async_copy(own, own_out, out_sems.at[1])
     back_copy = pltpu.make_async_copy(back, back_out, out_sems.at[2])
@@ -359,33 +371,43 @@
     part[...] = jnp.zeros_like(part)
 
     def cross_next(piece, level):
-        part[0, : ROOM[level], :] += dot_nt(
+        return dot_nt(
             from_next[piece, FIRST[level] : FIRST[level] + ROOM[level], :],
             stack[piece, DEPTH + level],
         )
 
     def cross_prev(piece, level):
-        part[1, : ROOM[level], :] += dot_nt(
+        return dot_nt(
             from_prev[piece, FIRST[level] : FIRST[level] + ROOM[level], :],
             stack[piece, DEPTH - 2 - level],
         )
 
+    def add_levels(direction, products):
+        edge = 0
+        for level in range(LEVELS - 1):
+            total = part[direction, edge : ROOM[level], :]
+            for other in products[level:]:
+                total += other[edge : ROOM[level]]
+            part[direction, edge : ROOM[level], :] = total
+            edge = ROOM[level]
+
     def cross_piece(piece, carry):
         @pl.when(piece < UP_PIECES)
         def _():
-            planes_up_copy(piece, MANY).wait()
-            planes_down_copy(piece, FEW).wait()
-            cross_next(piece, LEVELS - 1)
+            planes_up_copy(piece, MANY).wait_recv()
+            planes_down_copy(piece, FEW).wait_recv()
+            part[0, : ROOM[LEVELS - 1], :] += cross_next(piece, LEVELS - 1)
 
         @pl.when(piece >= UP_PIECES)
         def _():
-            planes_up_copy(piece, FEW).wait()
-            planes_down_copy(piece, MANY).wait()
-            cross_prev(piece, LEVELS - 1)
-
-        for level in range(LEVELS - 1):
-            cross_next(piece, level)
-            cross_prev(piece, level)
+            planes_up_copy(piece, FEW).wait_recv()
+            planes_down_copy(piece, MANY).wait_recv()
+            part[1, : ROOM[LEVELS - 1], :] += cross_prev(piece, LEVELS - 1)
+
+        with_next = [cross_next(piece, level) for level in range(LEVELS - 1)]
+        with_prev = [cross_prev(piece, level) for level in range(LEVELS - 1)]
+        add_levels(0, with_next)
+        add_levels(1, with_prev)
         return carry
 
     lax.fori_loop(0, PIECES, cross_piece, 0)
@@ -412,11 +434,16 @@
     own_copy.wait()
     back_copy.wait()
     side_copy.wait()
+    for piece in range(PIECES):
+        down_copy(piece).wait_send()
+        up_copy(piece).wait_send()
+        planes_up_copy(piece, MANY if piece < UP_PIECES else FEW).wait_send()
+        planes_down_copy(piece, FEW if piece < UP_PIECES else MANY).wait_send()
     part_to_next.wait()
     part_to_prev.wait()
 
 
-def finish_kernel(scale, rho, own, side, part_in, back, rho_out, ham_out, ovl_out):
+def finish_kernel(scale, side, part_in, rho, own, back, rho_out, ham_out, ovl_out):
     rho_out[...] = rho[...]
     none = jnp.zeros((SLOTS - PARTS, 2 * SLOTS), F32)
     from_prev = select_rows(back[0], jnp.concatenate([part_in[0], none], axis=0))
@@ -812,7 +839,7 @@
     )
 
     def as_sent():
-        return side, part_in
+        return side, part_in, rho, own, back
 
     def in_full():
         whole = full_call(
@@ -823,9 +850,9 @@
             nucleus_charge,
             applied_field,
         )
-        return whole, jnp.zeros_like(part_in)
-
-    side_blocks, received = lax.cond(over[0] > 0.0, in_full, as_sent)
+        return whole, jnp.zeros_like(part_in), rho, own, back
+
+    given = lax.cond(over[0] > 0.0, in_full, as_sent)
     return tuple(
         pl.pallas_call(
             functools.partial(finish_kernel, 1.0 / (depth * points)),
@@ -834,7 +861,7 @@
                 jax.ShapeDtypeStruct((slots, 3 * slots), F32),
                 jax.ShapeDtypeStruct((slots, 3 * slots), F32),
             ),
-        )(rho, own, side_blocks, received, back)
+        )(*given)
     )
 
 

time: 33.7 us -> 34.9 us (1.036)
  Pallas kernels: 32.2 us -> 33.4 us
    pallas_call x1, Pallas kernels: 30.3 us -> 31.5 us  [per_device(): pl.pallas_call(functools.partial(packed_kernel, count), out_shape=(jax.Sh...]
where the time goes in v3:
time: 34.9 us; the launch traced here: 34.7 us
  Pallas kernels  33.4 us (96%)
  between operations  1.35 us (4%)
    pallas_call x1, Pallas kernels, per_device(): pl.pallas_call(functools.partial(packed_kernel, count), out_shape=(jax.Sh...  31.5 us
    pallas_call x1, Pallas kernels, per_device(): pl.pallas_call(functools.partial(finish_kernel, 1.0 / (depth * points)),...  1.9 us

profile of v3, /device:TPU:0, one launch (start us, length us, event | category | flops | bytes accessed | tf_op | source)
XLA Modules:
  0.0 34.7 jit_solution(4221925784309898851)
XLA Ops:
  0.6 0.0 copy-start
  0.6 0.0 copy-start.1
  0.7 0.0 copy-start.2
  0.7 0.0 copy-start.3
  0.7 0.0 copy-start.4
  0.7 31.5 %shard_map.85 = (f32[8,2048]{1,0:T(8,128)}, f32[128,256]{1,0:T(8,128)}, f32[2,256,128]{2,1,0:T(8,128)S(1)}, f32[2,96,256]{2,1,0:T(8,128)S(1)}, bf16[2,128,128]{2,1,0:T(8,128)(2,1)}, /*index=5*/f32[1]{0:T(128)}) custom-call(bf16[1024,2048]{1,0:T(8,128)(2,1)} %bitcast.8, f32[1,128]{1,0:T(1,128)} %bitcast.12, s32[1,128]{1,0:T(1,128)} %bitcast.14, ...), custom_call_target="tpu_custom_call" | custom-call | flops 4000000000 | bytes 5242880 | tf_op jit(solution)/shard_map/pallas_call | solution.py:778
  32.8 0.0 copy-done
  32.8 0.0 copy-done.1
  32.8 0.0 copy-done.2
  32.8 0.0 copy-done.3
  32.8 0.0 copy-done.4
  32.8 1.9 %shard_map.86 = (f32[8,2048]{1,0:T(8,128)}, f32[128,384]{1,0:T(8,128)}, f32[128,384]{1,0:T(8,128)}) custom-call(f32[2,256,128]{2,1,0:T(8,128)S(1)} %get-tuple-element.36.side, f32[2,96,256]{2,1,0:T(8,128)S(1)} %get-tuple-element.37.part_in, f32[8,2048]{1,0:T(8,128)} %get-tuple-element.38.rho, f32[128,256]{1,0:T(8,128)} %get-tuple-element.39.own, ...), custom_call_target="tpu_custom_call" | custom-call | tf_op jit(solution)/shard_map/pallas_call | solution.py:857
  (1 shorter events, 0.0 us)
Async XLA Ops:
  0.6 32.1 %copy-start = (s32[16384]{0:T(1024)S(1)}, s32[16384]{0:T(1024)}, u32[]{:S(2)}) copy-start(s32[16384]{0:T(1024)} %param.11) | copy-start | bytes 196612
  0.6 32.1 %copy-start.1 = (f32[8,2048]{1,0:T(8,128)S(1)}, f32[8,2048]{1,0:T(8,128)}, u32[]{:S(2)}) copy-start(f32[8,2048]{1,0:T(8,128)} %nucleus_in.1) | copy-start | bytes 196612
  0.7 32.1 %copy-start.2 = (f32[8,2048]{1,0:T(8,128)S(1)}, f32[8,2048]{1,0:T(8,128)}, u32[]{:S(2)}) copy-start(f32[8,2048]{1,0:T(8,128)} %applied_in.1) | copy-start | bytes 196612
  0.7 32.1 %copy-start.3 = (f32[128]{0:T(128)S(1)}, f32[128]{0:T(128)}, u32[]{:S(2)}) copy-start(f32[128]{0:T(128)} %param.9) | copy-start | bytes 1540
  0.7 32.1 %copy-start.4 = (s32[128]{0:T(128)S(1)}, s32[128]{0:T(128)}, u32[]{:S(2)}) copy-start(s32[128]{0:T(128)} %param.10) | copy-start | bytes 1540

commit v4 on v3

--- a/solution.py
+++ b/solution.py
@@ -21,9 +21,9 @@
 ROOM = (32, 64, 80, 96)
 FIRST = (0, 32, 96, 176)
 FEW, MANY = 176, 272
-PARTS = 96
+PARTS = (80, 96)
 LAYERS = 4
-UP_PIECES = 1
+UP_PIECES = 0
 
 
 def dot_nt(a, b):
@@ -113,6 +113,9 @@
     me = lax.axis_index("func")
     following = lax.rem(me + 1, count)
     preceding = lax.rem(me + count - 1, count)
+    barrier = pltpu.get_barrier_semaphore()
+    for neighbour in (preceding, following):
+        pl.semaphore_signal(barrier, inc=1, device_id=(neighbour,), device_id_type=MESH)
     width = raw.shape[2]
     step = min(width, 256)
 
@@ -141,9 +144,6 @@
     for piece in range(PIECES):
         raw_copy(piece).start()
 
-    barrier = pltpu.get_barrier_semaphore()
-    for neighbour in (preceding, following):
-        pl.semaphore_signal(barrier, inc=1, device_id=(neighbour,), device_id_type=MESH)
     for copy in small:
         copy.wait()
 
@@ -359,15 +359,6 @@
         own_planes(piece, range(DEPTH, PLANES))
         return carry
 
-    lax.fori_loop(0, PIECES, low_planes, 0)
-    lax.fori_loop(0, PIECES, high_planes, 0)
-    rho_copy = pltpu.make_async_copy(rho, rho_out, out_sems.at[0])
-    own_copy = pltpu.make_async_copy(own, own_out, out_sems.at[1])
-    back_copy = pltpu.make_async_copy(back, back_out, out_sems.at[2])
-    rho_copy.start()
-    own_copy.start()
-    back_copy.start()
-
     part[...] = jnp.zeros_like(part)
 
     def cross_next(piece, level):
@@ -391,31 +382,73 @@
             part[direction, edge : ROOM[level], :] = total
             edge = ROOM[level]
 
-    def cross_piece(piece, carry):
+    odd = lax.rem(me, 2) == 1
+
+    def products_with_next(piece):
         @pl.when(piece < UP_PIECES)
         def _():
             planes_up_copy(piece, MANY).wait_recv()
+            part[0, : ROOM[LEVELS - 1], :] += cross_next(piece, LEVELS - 1)
+
+        @pl.when(piece >= UP_PIECES)
+        def _():
+            planes_up_copy(piece, FEW).wait_recv()
+
+        add_levels(0, [cross_next(piece, level) for level in range(LEVELS - 1)])
+
+    def products_with_previous(piece):
+        @pl.when(piece < UP_PIECES)
+        def _():
             planes_down_copy(piece, FEW).wait_recv()
-            part[0, : ROOM[LEVELS - 1], :] += cross_next(piece, LEVELS - 1)
 
         @pl.when(piece >= UP_PIECES)
         def _():
-            planes_up_copy(piece, FEW).wait_recv()
             planes_down_copy(piece, MANY).wait_recv()
             part[1, : ROOM[LEVELS - 1], :] += cross_prev(piece, LEVELS - 1)
 
-        with_next = [cross_next(piece, level) for level in range(LEVELS - 1)]
-        with_prev = [cross_prev(piece, level) for level in range(LEVELS - 1)]
-        add_levels(0, with_next)
-        add_levels(1, with_prev)
+        add_levels(1, [cross_prev(piece, level) for level in range(LEVELS - 1)])
+
+    def cross_piece(piece):
+        @pl.when(odd)
+        def _():
+            products_with_previous(piece)
+            products_with_next(piece)
+
+        @pl.when(jnp.logical_not(odd))
+        def _():
+            products_with_next(piece)
+            products_with_previous(piece)
+
+    @pl.when(odd)
+    def _():
+        lax.fori_loop(0, PIECES, low_planes, 0)
+
+    @pl.when(jnp.logical_not(odd))
+    def _():
+        lax.fori_loop(0, PIECES, high_planes, 0)
+
+    def other_planes(piece, carry):
+        @pl.when(odd)
+        def _():
+            high_planes(piece, 0)
+
+        @pl.when(jnp.logical_not(odd))
+        def _():
+            low_planes(piece, 0)
+
+        @pl.when(piece > 0)
+        def _():
+            cross_piece(piece - 1)
+
         return carry
 
-    lax.fori_loop(0, PIECES, cross_piece, 0)
+    lax.fori_loop(0, PIECES, other_planes, 0)
+    cross_piece(jnp.int32(PIECES - 1))
 
     def part_copy(which, target):
         return pltpu.make_async_remote_copy(
-            src_ref=part.at[which, pl.ds(0, PARTS)],
-            dst_ref=part_in.at[which],
+            src_ref=part.at[which, pl.ds(0, PARTS[which])],
+            dst_ref=part_in.at[which, pl.ds(0, PARTS[which])],
             send_sem=part_sems.at[0, which],
             recv_sem=part_sems.at[1, which],
             device_id=(target,),
@@ -426,6 +459,12 @@
     part_to_prev = part_copy(1, preceding)
     part_to_next.start()
     part_to_prev.start()
+    rho_copy = pltpu.make_async_copy(rho, rho_out, out_sems.at[0])
+    own_copy = pltpu.make_async_copy(own, own_out, out_sems.at[1])
+    back_copy = pltpu.make_async_copy(back, back_out, out_sems.at[2])
+    rho_copy.start()
+    own_copy.start()
+    back_copy.start()
     side[0] = select_columns(part[0].T, up_matrix(following).astype(BF16))
     side[1] = select_columns(part[1].T, down_matrix(preceding).astype(BF16))
     side_copy = pltpu.make_async_copy(side, side_out, out_sems.at[3])
@@ -445,9 +484,13 @@
 
 def finish_kernel(scale, side, part_in, rho, own, back, rho_out, ham_out, ovl_out):
     rho_out[...] = rho[...]
-    none = jnp.zeros((SLOTS - PARTS, 2 * SLOTS), F32)
-    from_prev = select_rows(back[0], jnp.concatenate([part_in[0], none], axis=0))
-    from_next = select_rows(back[1], jnp.concatenate([part_in[1], none], axis=0))
+
+    def rows_of(which):
+        none = jnp.zeros((SLOTS - PARTS[which], 2 * SLOTS), F32)
+        return select_rows(back[which], jnp.concatenate([part_in[which, : PARTS[which]], none], axis=0))
+
+    from_prev = rows_of(0)
+    from_next = rows_of(1)
     ovl_out[:, :SLOTS] = (side[1, :SLOTS, :] + from_prev[:, :SLOTS]) * scale
     ham_out[:, :SLOTS] = (side[1, SLOTS:, :] + from_prev[:, SLOTS:]) * scale
     ovl_out[:, SLOTS : 2 * SLOTS] = own[:, :SLOTS] * scale
@@ -781,7 +824,7 @@
             jax.ShapeDtypeStruct((depth, points), F32),
             jax.ShapeDtypeStruct((slots, 2 * slots), F32),
             jax.ShapeDtypeStruct((2, 2 * slots, slots), F32),
-            jax.ShapeDtypeStruct((2, PARTS, 2 * slots), F32),
+            jax.ShapeDtypeStruct((2, max(PARTS), 2 * slots), F32),
             jax.ShapeDtypeStruct((2, slots, slots), BF16),
             jax.ShapeDtypeStruct((1,), F32),
         ),

time: 34.9 us -> 32.9 us (0.943)
  Pallas kernels: 33.4 us -> 31.4 us
    pallas_call x1, Pallas kernels: 31.5 us -> 29.4 us  [per_device(): pl.pallas_call(functools.partial(packed_kernel, count), out_shape=(jax.Sh...]
where the time goes in v4:
time: 32.9 us; the launch traced here: 32.7 us
  Pallas kernels  31.4 us (95%)
  between operations  1.35 us (4%)
    pallas_call x1, Pallas kernels, per_device(): pl.pallas_call(functools.partial(packed_kernel, count), out_shape=(jax.Sh...  29.4 us
    pallas_call x1, Pallas kernels, per_device(): pl.pallas_call(functools.partial(finish_kernel, 1.0 / (depth * points)),...  1.91 us

profile of v4, /device:TPU:0, one launch (start us, length us, event | category | flops | bytes accessed | tf_op | source)
XLA Modules:
  0.0 32.7 jit_solution(3756818066272442054)
XLA Ops:
  0.6 0.0 copy-start
  0.6 0.0 copy-start.1
  0.7 0.0 copy-start.2
  0.7 0.0 copy-start.3
  0.7 0.0 copy-start.4
  0.7 29.4 %shard_map.85 = (f32[8,2048]{1,0:T(8,128)}, f32[128,256]{1,0:T(8,128)}, f32[2,256,128]{2,1,0:T(8,128)S(1)}, f32[2,96,256]{2,1,0:T(8,128)S(1)}, bf16[2,128,128]{2,1,0:T(8,128)(2,1)}, /*index=5*/f32[1]{0:T(128)}) custom-call(bf16[1024,2048]{1,0:T(8,128)(2,1)} %bitcast.8, f32[1,128]{1,0:T(1,128)} %bitcast.12, s32[1,128]{1,0:T(1,128)} %bitcast.14, ...), custom_call_target="tpu_custom_call" | custom-call | flops 4000000000 | bytes 5242880 | tf_op jit(solution)/shard_map/pallas_call | solution.py:821
  30.8 0.0 copy-done
  30.8 0.0 copy-done.1
  30.8 0.0 copy-done.2
  30.8 0.0 copy-done.3
  30.8 0.0 copy-done.4
  30.8 1.9 %shard_map.86 = (f32[8,2048]{1,0:T(8,128)}, f32[128,384]{1,0:T(8,128)}, f32[128,384]{1,0:T(8,128)}) custom-call(f32[2,256,128]{2,1,0:T(8,128)S(1)} %get-tuple-element.36.side, f32[2,96,256]{2,1,0:T(8,128)S(1)} %get-tuple-element.37.part_in, f32[8,2048]{1,0:T(8,128)} %get-tuple-element.38.rho, f32[128,256]{1,0:T(8,128)} %get-tuple-element.39.own, ...), custom_call_target="tpu_custom_call" | custom-call | tf_op jit(solution)/shard_map/pallas_call | solution.py:900
  (1 shorter events, 0.0 us)
Async XLA Ops:
  0.6 30.1 %copy-start = (s32[16384]{0:T(1024)S(1)}, s32[16384]{0:T(1024)}, u32[]{:S(2)}) copy-start(s32[16384]{0:T(1024)} %param.11) | copy-start | bytes 196612
  0.6 30.1 %copy-start.1 = (f32[8,2048]{1,0:T(8,128)S(1)}, f32[8,2048]{1,0:T(8,128)}, u32[]{:S(2)}) copy-start(f32[8,2048]{1,0:T(8,128)} %nucleus_in.1) | copy-start | bytes 196612
  0.7 30.1 %copy-start.2 = (f32[8,2048]{1,0:T(8,128)S(1)}, f32[8,2048]{1,0:T(8,128)}, u32[]{:S(2)}) copy-start(f32[8,2048]{1,0:T(8,128)} %applied_in.1) | copy-start | bytes 196612
  0.7 30.1 %copy-start.3 = (f32[128]{0:T(128)S(1)}, f32[128]{0:T(128)}, u32[]{:S(2)}) copy-start(f32[128]{0:T(128)} %param.9) | copy-start | bytes 1540
  0.7 30.1 %copy-start.4 = (s32[128]{0:T(128)S(1)}, s32[128]{0:T(128)}, u32[]{:S(2)}) copy-start(s32[128]{0:T(128)} %param.10) | copy-start | bytes 1540
